TPU v7x, 32 devices: a whole 2x2x4 slice. The times are simulated.
32 devices in a mesh: fsdp: 4 (over y, core), ctx: 4 (over z), tp: 2 (over x).
Axes of the slice: x: 2, y: 2, z: 4, core: 2. Of those that a mesh axis runs over, the one named last changes fastest.
Arguments:
- tokens: bfloat16 [8, 2048, 960], P('fsdp', ('ctx', 'tp')), may hold values from -6 to 6
- cotangent: bfloat16 [8, 2048, 960], P('fsdp', ('ctx', 'tp')), may hold values from -6 to 6
- input_gain: bfloat16 [960], P('fsdp'), may hold values from 0.099609375 to 1.8984375
- w_query: bfloat16 [960, 960], P('fsdp'), may hold values from -0.1875 to 0.1875
- w_keyval: bfloat16 [960, 640], P('fsdp'), may hold values from -0.1875 to 0.1875
- w_output: bfloat16 [960, 960], P('fsdp'), may hold values from -2 to 2
- middle_gain: bfloat16 [960], P('fsdp'), may hold values from 0.099609375 to 1.8984375
- w_gate: bfloat16 [960, 2560], P('fsdp', 'tp'), may hold values from -0.1875 to 0.1875
- w_up: bfloat16 [960, 2560], P('fsdp', 'tp'), may hold values from -0.1875 to 0.1875
- w_down: bfloat16 [960, 2560], P('fsdp', 'tp'), may hold values from -0.25 to 0.25
Outputs:
- result: bfloat16 [8, 2048, 960], P('fsdp', ('ctx', 'tp'))
- grad_tokens: float32 [8, 2048, 960], P('fsdp', ('ctx', 'tp'))
- grad_input_gain: float32 [960], P('fsdp')
- grad_w_query: float32 [960, 960], P('fsdp')
- grad_w_keyval: float32 [960, 640], P('fsdp')
- grad_w_output: float32 [960, 960], P('fsdp')
- grad_middle_gain: float32 [960], P('fsdp')
- grad_w_gate: float32 [960, 2560], P('fsdp', 'tp')
- grad_w_up: float32 [960, 2560], P('fsdp', 'tp')
- grad_w_down: float32 [960, 2560], P('fsdp', 'tp')
All inputs are finite; a program needn't handle non-finite values.
Results may differ from a plain program's by a relative error of at most 0.02.
Values may be sent and summed in bfloat16 or wider, within the bound.
A program may use at most 128 MiB of HBM per device.

v0:
```python
from functools import partial
import jax
import jax.numpy as jnp
from jax import lax
from jax.sharding import PartitionSpec as P

QUERY_HEADS = 15
KEYVAL_HEADS = 5
HEAD_WIDTH = 64
SEQUENCE_LENGTH = 2048
KEY_WIDTH = 320
EPS = 1e-05
THETA = 10000.0


def rope_tables(token_positions, first_place):
    half_width = HEAD_WIDTH // 2
    position = (first_place + lax.iota(jnp.int32, token_positions)).astype(jnp.float32)
    frequency = THETA ** (-(2.0 * lax.iota(jnp.int32, half_width).astype(jnp.float32)) / HEAD_WIDTH)
    angles = position[:, None] * frequency[None, :]
    return (jnp.cos(angles), jnp.sin(angles))


def apply_rotary(value_rows, cosine_table, sine_table, heads):
    half_width = HEAD_WIDTH // 2
    shaped = value_rows.reshape(value_rows.shape[:-1] + (heads, HEAD_WIDTH))
    leading = shaped[..., :half_width]
    trailing = shaped[..., half_width:]
    cosine_wide = cosine_table[:, None, :]
    sine_wide = sine_table[:, None, :]
    turned = jnp.concatenate(
        [
            leading * cosine_wide - trailing * sine_wide,
            trailing * cosine_wide + leading * sine_wide,
        ],
        -1,
    )
    return turned.reshape(value_rows.shape)


def normalize(value_rows):
    inverse_rms = lax.rsqrt(jnp.mean(value_rows * value_rows, -1, keepdims=True) + EPS)
    return (value_rows * inverse_rms, inverse_rms)


def norm_back(back_unit, unit_rows, inverse_rms):
    return inverse_rms * (
        back_unit - unit_rows * jnp.mean(back_unit * unit_rows, -1, keepdims=True)
    )


def to_heads(value_rows, sequence_count, token_positions):
    group_total = QUERY_HEADS // KEYVAL_HEADS
    return (
        value_rows.reshape(sequence_count, token_positions, KEYVAL_HEADS, group_total, HEAD_WIDTH)
        .transpose(0, 2, 3, 1, 4)
        .reshape(sequence_count * KEYVAL_HEADS, group_total * token_positions, HEAD_WIDTH)
    )


def from_heads(value_rows, sequence_count, token_positions):
    group_total = QUERY_HEADS // KEYVAL_HEADS
    return (
        value_rows.reshape(sequence_count, KEYVAL_HEADS, group_total, token_positions, HEAD_WIDTH)
        .transpose(0, 3, 1, 2, 4)
        .reshape(sequence_count, token_positions, QUERY_HEADS * HEAD_WIDTH)
    )


def per_sequence(value_rows, sequence_count):
    return value_rows.reshape((sequence_count, KEYVAL_HEADS) + value_rows.shape[1:])


def masked_scores(query_group, key_group, allowed):
    raw_scores = jnp.einsum("qd,kd->qk", query_group, key_group, preferred_element_type=jnp.float32)
    return jnp.where(allowed, raw_scores * HEAD_WIDTH ** (-0.5), -jnp.inf)


def head_forward(head_items, allowed):
    query_group, key_group, value_group = head_items
    scores = masked_scores(query_group, key_group, allowed)
    row_top = jnp.max(scores, -1, keepdims=True)
    lifted = jnp.exp(scores - row_top)
    row_total = jnp.sum(lifted, -1, keepdims=True)
    weights = (lifted / row_total).astype(jnp.bfloat16)
    mixed_heads = jnp.einsum("qk,kd->qd", weights, value_group, preferred_element_type=jnp.float32)
    return (mixed_heads, row_top[:, 0], row_total[:, 0])


def head_backward(head_items, allowed):
    query_group, key_group, value_group, back_mixed, row_top, row_total = head_items
    scores = masked_scores(query_group, key_group, allowed)
    weights = jnp.exp(scores - row_top[:, None]) / row_total[:, None]
    back_weights = jnp.einsum(
        "qd,kd->qk", back_mixed, value_group, preferred_element_type=jnp.float32
    )
    weighted_sum = jnp.sum(weights * back_weights, -1, keepdims=True)
    back_scores = (weights * (back_weights - weighted_sum)).astype(jnp.bfloat16)
    back_query = jnp.einsum(
        "qk,kd->qd", back_scores, key_group, preferred_element_type=jnp.float32
    ) * HEAD_WIDTH ** (-0.5)
    back_key = jnp.einsum(
        "qk,qd->kd", back_scores, query_group, preferred_element_type=jnp.float32
    ) * HEAD_WIDTH ** (-0.5)
    back_value = jnp.einsum(
        "qk,qd->kd", weights.astype(jnp.bfloat16), back_mixed, preferred_element_type=jnp.float32
    )
    return (back_query, back_key, back_value)


def on_device(
    tokens, cotangent, input_gain, w_query, w_keyval, w_output, middle_gain, w_gate, w_up, w_down
):
    sequence_count = tokens.shape[0]
    token_positions = tokens.shape[1]
    group_total = QUERY_HEADS // KEYVAL_HEADS
    place_index = lax.axis_index("ctx") * lax.axis_size("tp") + lax.axis_index("tp")
    first_place = place_index * token_positions
    cosine_table, sine_table = rope_tables(token_positions, first_place)
    query_place = first_place + lax.iota(jnp.int32, group_total * token_positions) % token_positions
    allowed = lax.iota(jnp.int32, SEQUENCE_LENGTH)[None, :] <= query_place[:, None]
    full_gain_one, full_query, full_keyval, full_output = (
        lax.all_gather(input_gain, "fsdp", axis=0, tiled=True),
        lax.all_gather(w_query, "fsdp", axis=0, tiled=True),
        lax.all_gather(w_keyval, "fsdp", axis=0, tiled=True),
        lax.all_gather(w_output, "fsdp", axis=0, tiled=True),
    )
    gain_one = full_gain_one.astype(jnp.float32)
    inputs = tokens.astype(jnp.float32)
    unit_one, inverse_one = normalize(inputs)
    normed_one = (unit_one * gain_one).astype(jnp.bfloat16)
    query_raw = jnp.dot(normed_one, full_query, preferred_element_type=jnp.float32)
    keyval_unrotated = jnp.dot(normed_one, full_keyval, preferred_element_type=jnp.float32)
    query_low = apply_rotary(query_raw, cosine_table, sine_table, QUERY_HEADS).astype(jnp.bfloat16)
    keyval_low = jnp.concatenate(
        [
            apply_rotary(keyval_unrotated[..., :KEY_WIDTH], cosine_table, sine_table, KEYVAL_HEADS),
            keyval_unrotated[..., KEY_WIDTH:],
        ],
        -1,
    ).astype(jnp.bfloat16)
    keyval_gathered = lax.all_gather(keyval_low, ("ctx", "tp"), axis=1, tiled=True)
    query_heads = to_heads(query_low, sequence_count, token_positions)
    stacked = (
        keyval_gathered.reshape(sequence_count, SEQUENCE_LENGTH, 2, KEYVAL_HEADS, HEAD_WIDTH)
        .transpose(2, 0, 3, 1, 4)
        .reshape(2, sequence_count * KEYVAL_HEADS, SEQUENCE_LENGTH, HEAD_WIDTH)
    )
    key_heads = stacked[0]
    value_heads = stacked[1]
    mixed_heads, row_top, row_total = lax.map(
        partial(head_forward, allowed=allowed), (query_heads, key_heads, value_heads)
    )
    mixed_low = from_heads(mixed_heads, sequence_count, token_positions).astype(jnp.bfloat16)
    attention_out = jnp.dot(mixed_low, full_output, preferred_element_type=jnp.float32)
    middle = inputs + attention_out
    full_gate, full_up, full_down, full_gain_two = (
        lax.all_gather(w_gate, "fsdp", axis=0, tiled=True),
        lax.all_gather(w_up, "fsdp", axis=0, tiled=True),
        lax.all_gather(w_down, "fsdp", axis=0, tiled=True),
        lax.all_gather(middle_gain, "fsdp", axis=0, tiled=True),
    )
    gain_two = full_gain_two.astype(jnp.float32)
    unit_two, inverse_two = normalize(middle)
    normed_two = (unit_two * gain_two).astype(jnp.bfloat16)
    pair_rows, pair_cotangent = (
        lax.all_gather(normed_two, "tp", axis=1, tiled=True),
        lax.all_gather(cotangent, "tp", axis=1, tiled=True),
    )
    gate_proj = jnp.dot(pair_rows, full_gate, preferred_element_type=jnp.float32)
    up_proj = jnp.dot(pair_rows, full_up, preferred_element_type=jnp.float32)
    sigmoid_gate = jax.nn.sigmoid(gate_proj)
    swish_gate = gate_proj * sigmoid_gate
    hidden = (swish_gate * up_proj).astype(jnp.bfloat16)
    branch_part = jnp.einsum("spf,df->spd", hidden, full_down, preferred_element_type=jnp.float32)
    feed_out = lax.psum_scatter(
        branch_part.astype(jnp.bfloat16), "tp", scatter_dimension=1, tiled=True
    ).astype(jnp.float32)
    result = (middle + feed_out).astype(jnp.bfloat16)
    back_hidden = jnp.dot(pair_cotangent, full_down, preferred_element_type=jnp.float32)
    back_gate = (
        back_hidden * up_proj * sigmoid_gate * (1.0 + gate_proj * (1.0 - sigmoid_gate))
    ).astype(jnp.bfloat16)
    back_up = (back_hidden * swish_gate).astype(jnp.bfloat16)
    grad_down = jnp.einsum(
        "spd,spf->df", pair_cotangent, hidden, preferred_element_type=jnp.float32
    )
    grad_gate = jnp.einsum("spd,spf->df", pair_rows, back_gate, preferred_element_type=jnp.float32)
    grad_up = jnp.einsum("spd,spf->df", pair_rows, back_up, preferred_element_type=jnp.float32)
    back_normed_part = jnp.einsum(
        "spf,df->spd", back_gate, full_gate, preferred_element_type=jnp.float32
    ) + jnp.einsum("spf,df->spd", back_up, full_up, preferred_element_type=jnp.float32)
    back_normed_two = lax.psum_scatter(back_normed_part, "tp", scatter_dimension=1, tiled=True)
    grad_gain_two = jnp.sum(back_normed_two * unit_two, axis=(0, 1))
    back_middle = cotangent.astype(jnp.float32) + norm_back(
        back_normed_two * gain_two, unit_two, inverse_two
    )
    back_attention = back_middle.astype(jnp.bfloat16)
    grad_output = jnp.einsum(
        "spq,spd->qd", mixed_low, back_attention, preferred_element_type=jnp.float32
    )
    back_mixed = jnp.einsum(
        "spd,qd->spq", back_attention, full_output, preferred_element_type=jnp.float32
    ).astype(jnp.bfloat16)

    def attend_back(carried, sequence_items):
        back_query, back_key, back_value = lax.map(
            partial(head_backward, allowed=allowed), sequence_items
        )
        back_keyval = (
            jnp.stack([back_key, back_value])
            .transpose(2, 0, 1, 3)
            .reshape(SEQUENCE_LENGTH, 2 * KEY_WIDTH)
        )
        owned_rows = lax.psum_scatter(
            back_keyval.astype(jnp.bfloat16), ("ctx", "tp"), scatter_dimension=0, tiled=True
        ).astype(jnp.float32)
        return (carried, (back_query, owned_rows))

    sequence_items = tuple(
        (
            per_sequence(value_rows, sequence_count)
            for value_rows in (
                query_heads,
                key_heads,
                value_heads,
                to_heads(back_mixed, sequence_count, token_positions),
                row_top,
                row_total,
            )
        )
    )
    unused, (query_gradient_full, owned_tokens_full) = lax.scan(
        attend_back, jnp.zeros((), jnp.float32), sequence_items
    )
    back_query_rows = from_heads(
        query_gradient_full.reshape(
            (sequence_count * KEYVAL_HEADS,) + query_gradient_full.shape[2:]
        ),
        sequence_count,
        token_positions,
    )
    back_query_low = apply_rotary(back_query_rows, cosine_table, -sine_table, QUERY_HEADS).astype(
        jnp.bfloat16
    )
    back_keyval_low = jnp.concatenate(
        [
            apply_rotary(
                owned_tokens_full[..., :KEY_WIDTH], cosine_table, -sine_table, KEYVAL_HEADS
            ),
            owned_tokens_full[..., KEY_WIDTH:],
        ],
        -1,
    ).astype(jnp.bfloat16)
    grad_query = jnp.einsum(
        "spd,spq->dq", normed_one, back_query_low, preferred_element_type=jnp.float32
    )
    grad_keyval = jnp.einsum(
        "spd,spk->dk", normed_one, back_keyval_low, preferred_element_type=jnp.float32
    )
    back_normed_one = jnp.einsum(
        "spq,dq->spd", back_query_low, full_query, preferred_element_type=jnp.float32
    ) + jnp.einsum("spk,dk->spd", back_keyval_low, full_keyval, preferred_element_type=jnp.float32)
    grad_gain_one = jnp.sum(back_normed_one * unit_one, axis=(0, 1))
    back_inputs = back_middle + norm_back(back_normed_one * gain_one, unit_one, inverse_one)
    attention_term = jnp.concatenate([grad_query, grad_keyval, grad_output], 1)
    feed_term = jnp.concatenate([grad_gate, grad_up, grad_down], 1)
    attention_total, gain_one_total, gain_two_total = (
        lax.psum(attention_term.astype(jnp.bfloat16), ("ctx", "tp")).astype(jnp.float32),
        lax.psum(grad_gain_one.astype(jnp.bfloat16), ("ctx", "tp")).astype(jnp.float32),
        lax.psum(grad_gain_two.astype(jnp.bfloat16), ("ctx", "tp")).astype(jnp.float32),
    )
    feed_total = lax.psum(feed_term.astype(jnp.bfloat16), "ctx")
    attention_share, feed_share, gain_one_share, gain_two_share = (
        lax.psum_scatter(
            attention_total.astype(jnp.bfloat16), "fsdp", scatter_dimension=0, tiled=True
        ).astype(jnp.float32),
        lax.psum_scatter(feed_total, "fsdp", scatter_dimension=0, tiled=True).astype(jnp.float32),
        lax.psum_scatter(
            gain_one_total.astype(jnp.bfloat16), "fsdp", scatter_dimension=0, tiled=True
        ).astype(jnp.float32),
        lax.psum_scatter(
            gain_two_total.astype(jnp.bfloat16), "fsdp", scatter_dimension=0, tiled=True
        ).astype(jnp.float32),
    )
    query_width = full_query.shape[1]
    keyval_width = full_keyval.shape[1]
    hidden_width = full_gate.shape[1]
    share_query = attention_share[:, :query_width]
    share_keyval = attention_share[:, query_width : query_width + keyval_width]
    share_output = attention_share[:, query_width + keyval_width :]
    share_gate = feed_share[:, :hidden_width]
    share_up = feed_share[:, hidden_width : 2 * hidden_width]
    share_down = feed_share[:, 2 * hidden_width :]
    return (
        result,
        back_inputs,
        gain_one_share,
        share_query,
        share_keyval,
        share_output,
        gain_two_share,
        share_gate,
        share_up,
        share_down,
    )


def solution(mesh):
    in_specs = (
        P("fsdp", ("ctx", "tp"), None),
        P("fsdp", ("ctx", "tp"), None),
        P("fsdp"),
        P("fsdp", None),
        P("fsdp", None),
        P("fsdp", None),
        P("fsdp"),
        P("fsdp", "tp"),
        P("fsdp", "tp"),
        P("fsdp", "tp"),
    )
    out_specs = (
        P("fsdp", ("ctx", "tp"), None),
        P("fsdp", ("ctx", "tp"), None),
        P("fsdp"),
        P("fsdp", None),
        P("fsdp", None),
        P("fsdp", None),
        P("fsdp"),
        P("fsdp", "tp"),
        P("fsdp", "tp"),
        P("fsdp", "tp"),
    )
    return jax.shard_map(
        on_device, mesh=mesh, in_specs=in_specs, out_specs=out_specs, check_vma=False
    )
```

profile of v0, /device:TPU:0, one launch (start us, length us, event | category | flops | bytes accessed | tf_op | source)
XLA Modules:
  0.0 1055.6 jit_solution(356635097389830232)
XLA Ops:
  12.4 8.3 all-reduce.6
  23.0 7.0 all-gather.12.cloned.1.call-done
  37.5 16.0 %all-gather.10.cloned.1.call-done = bf16[960,960]{1,0:T(8,128)(2,1)} async-done(((bf16[240,960]{1,0:T(8,128)(2,1)}), bf16[960,960]{1,0:T(8,128)(2,1)}) %all-gather.10.cloned.1.call-update) | async-done | bytes 1843216 | tf_op jit(solution)/shard_map/all_gather | solution.py:124
  58.6 84.0 %all-gather.14.cloned.1.call-done = bf16[2,2048,640]{2,1,0:T(8,128)(2,1)} async-done(((bf16[2,256,640]{2,1,0:T(8,128)(2,1)}), bf16[2,2048,640]{2,1,0:T(8,128)(2,1)}) %all-gather.14.cloned.1.call-update) | async-done | bytes 5242896 | tf_op jit(solution)/shard_map/all_gather | solution.py:142
  142.6 8.0 copy.72
  150.6 7.3 slice_bitcast_fusion
  157.9 80.6 %while.43 = (s32[]{:T(128)}, bf16[10,768,64]{1,2,0:T(8,128)(2,1)S(1)}, f32[10,768]{1,0:T(8,128)S(1)}, f32[10,768]{1,0:T(8,128)S(1)}, bf16[10,768,64]{2,1,0:T(8,1...) while((s32[]{:T(128)}, ...), condition=%wide.region_4.5_spmd.clone, body=%wide.region_1.4_spmd.clone.sunk | while | flops 426244608 | bytes 19846260 | solution.py:151
  170.4 3.4 fusion.152
  210.7 3.4 fusion.152
  248.7 7.6 fusion.58
  256.3 26.9 %all-gather.18.cloned.1.call-done = bf16[2,512,960]{1,2,0:T(8,128)(2,1)} async-done(((bf16[2,256,960]{1,2,0:T(8,128)(2,1)}), bf16[2,512,960]{1,2,0:T(8,128)(2,1)}) %all-gather.18.cloned.1.call-update) | async-done | bytes 1966096 | tf_op jit(solution)/shard_map/all_gather | solution.py:167
  283.1 7.6 fusion.64
  290.7 18.6 %all-gather.20.cloned.1.call-done = bf16[960,1280]{1,0:T(8,128)(2,1)} async-done(((bf16[240,1280]{1,0:T(8,128)(2,1)}), bf16[960,1280]{1,0:T(8,128)(2,1)}) %all-gather.20.cloned.1.call-update) | async-done | bytes 2457616 | tf_op jit(solution)/shard_map/all_gather | solution.py:158
  309.4 11.9 %multiply_convert_fusion.2 = (bf16[2,512,1280]{2,1,0:T(8,128)(2,1)S(1)}, bf16[2,512,1280]{2,1,0:T(8,128)(2,1)S(1)}, bf16[2,512,1280]{2,1,0:T(8,128)(2,1)}) fusion(f32[2,512,1280]{2,1,0:T(8,128)} %fusion.58, f32[2,512,1280]{2,1,0:T(8,128)} %fusion.64, bf16[2,512,960]{1,2,0:T(8,128)(2,1)} %all-gather.18.cloned.1.call-done, ...), kind=kOutput, calls=%fused_computation.71 | convolution fusion | flops 2536243200 | bytes 22773760 | tf_op jit(solution)/shard_map/dot_general | solution.py:170
  324.8 4.9 fusion.85
  329.8 6.5 fusion.88
  336.4 5.6 fusion.53
  342.0 3.4 bitcast_convert_fusion.2
  345.4 3.4 bitcast_convert_fusion.1
  348.9 3.4 pad_maximum_fusion.1
  352.3 29.6 %reduce-scatter.8.cloned.1.call-done = f32[2,256,960]{1,2,0:T(8,128)} async-done(((f32[2,512,960]{1,2,0:T(8,128)}), f32[2,256,960]{1,2,0:T(8,128)}) %reduce-scatter.8.cloned.1.call-update) | async-done | bytes 1966096 | tf_op jit(solution)/shard_map/reduce_scatter | solution.py:193
  384.5 30.1 %reduce-scatter.6.cloned.1.call-done = bf16[2,256,960]{1,2,0:T(8,128)(2,1)} async-done(((bf16[2,512,960]{1,2,0:T(8,128)(2,1)}), bf16[2,256,960]{1,2,0:T(8,128)(2,1)}) %reduce-scatter.6.cloned.1.call-update) | async-done | bytes 983056 | tf_op jit(solution)/shard_map/reduce_scatter | solution.py:176
  414.6 3.5 multiply_add_fusion
  421.2 340.2 %while.45 = (s32[]{:T(128)}, f32[2,5,768,64]{2,3,1,0:T(8,128)}, f32[2,256,640]{1,2,0:T(8,128)}, bf16[2,5,768,64]{3,2,1,0:T(8,128)(2,1)}, bf16[2,5,2048,64]{2,3,1...) while((s32[]{:T(128)}, f32[2,5,768,64]{2,3,1,0:T(8,128)}, ...), condition=%wide.region_14.15_spmd.clone, body=%wide.region_9.14_spmd.clone.sunk | while | flops 1025588480 | bytes 125203080 | solution.py:233
  435.6 79.8 %while.46 = (s32[]{:T(128)}, f32[5,768,64]{1,2,0:T(8,128)}, bf16[5,2048,64]{1,2,0:T(8,128)(2,1)}, bf16[5,2048,64]{1,2,0:T(8,128)(2,1)}, bf16[5,768,64]{2,1,0:T(8...) while((s32[]{:T(128)}, f32[5,768,64]{1,2,0:T(8,128)}, ...), condition=%wide.region_12.12_spmd, body=%wide.region_10.11_spmd.sunk | while | flops 1022541056 | bytes 79656208 | solution.py:207
  439.1 3.7 multiply_reduce_fusion.5
  455.1 3.7 multiply_reduce_fusion.5
  471.1 3.7 multiply_reduce_fusion.5
  487.0 3.7 multiply_reduce_fusion.5
  503.0 3.7 multiply_reduce_fusion.5
  515.4 3.5 pad_maximum_fusion.11
  521.2 68.9 %reduce-scatter.14.cloned.1.call-done = bf16[256,640]{0,1:T(8,128)(2,1)} async-done(((bf16[2048,640]{0,1:T(8,128)(2,1)}), bf16[256,640]{0,1:T(8,128)(2,1)}) %reduce-scatter.14.cloned.1.call-update) | async-done | bytes 327696 | tf_op jit(solution)/shard_map/while/body/eval_jaxpr/reduce_scatter | solution.py:215
  606.1 79.8 %while.46 = (s32[]{:T(128)}, f32[5,768,64]{1,2,0:T(8,128)}, bf16[5,2048,64]{1,2,0:T(8,128)(2,1)}, bf16[5,2048,64]{1,2,0:T(8,128)(2,1)}, bf16[5,768,64]{2,1,0:T(8...) while((s32[]{:T(128)}, f32[5,768,64]{1,2,0:T(8,128)}, ...), condition=%wide.region_12.12_spmd, body=%wide.region_10.11_spmd.sunk | while | flops 1022541056 | bytes 79656208 | solution.py:207
  609.7 3.7 multiply_reduce_fusion.5
  625.6 3.7 multiply_reduce_fusion.5
  641.6 3.7 multiply_reduce_fusion.5
  657.6 3.7 multiply_reduce_fusion.5
  673.5 3.7 multiply_reduce_fusion.5
  686.0 3.5 pad_maximum_fusion.11
  691.8 67.5 %reduce-scatter.14.cloned.1.call-done = bf16[256,640]{0,1:T(8,128)(2,1)} async-done(((bf16[2048,640]{0,1:T(8,128)(2,1)}), bf16[256,640]{0,1:T(8,128)(2,1)}) %reduce-scatter.14.cloned.1.call-update) | async-done | bytes 327696 | tf_op jit(solution)/shard_map/while/body/eval_jaxpr/reduce_scatter | solution.py:215
  779.7 9.3 concatenate.38
  789.1 40.0 %reduce-scatter.12.cloned.1.call-done = bf16[240,3840]{1,0:T(8,128)(2,1)} async-done(((bf16[960,3840]{1,0:T(8,128)(2,1)}), bf16[240,3840]{1,0:T(8,128)(2,1)}) %reduce-scatter.12.cloned.1.call-update) | async-done | bytes 1843216 | tf_op jit(solution)/shard_map/reduce_scatter | solution.py:278
  835.5 5.7 all-reduce.5
  841.4 21.5 %all-reduce.4 = (bf16[240]{0:T(256)(128)(2,1)S(1)}, bf16[240]{0:T(256)(128)(2,1)S(1)}) all-reduce(bf16[240]{0:T(256)(128)(2,1)S(1)} %dynamic-slice.3, bf16[240]{0:T(256)(128)(2,1)S(1)} %dynamic-slice.5), channel_id=1, replica_groups=mesh['fsdp'=4,'ctx'=4,'tp'=2] {'ctx','tp'}, use_global_device_ids=true, to_apply=%region_17.18 | all-reduce | flops 480 | bytes 1920 | tf_op jit(solution)/shard_map/psum | solution.py:270
  864.1 16.8 %reduce-scatter.10.cloned.1.call-done = bf16[240,2560]{1,0:T(8,128)(2,1)} async-done(((bf16[960,2560]{1,0:T(8,128)(2,1)}), bf16[240,2560]{1,0:T(8,128)(2,1)}) %reduce-scatter.10.cloned.1.call-update) | async-done | bytes 1228816 | tf_op jit(solution)/shard_map/reduce_scatter | solution.py:275
  884.3 77.4 %all-reduce.12.cloned.1.call-done = bf16[240,3840]{1,0:T(8,128)(2,1)} async-done(((bf16[240,3840]{1,0:T(8,128)(2,1)}), bf16[240,3840]{1,0:T(8,128)(2,1)}) %all-reduce.12.cloned.1.call-update) | async-done | bytes 1843216 | tf_op jit(solution)/shard_map/psum | solution.py:273
  961.7 3.4 fusion.112
  965.0 80.2 %all-reduce.10.cloned.1.call-done = bf16[240,2560]{1,0:T(8,128)(2,1)} async-done(((bf16[240,2560]{1,0:T(8,128)(2,1)}), bf16[240,2560]{1,0:T(8,128)(2,1)}) %all-reduce.10.cloned.1.call-update) | async-done | bytes 1228816 | tf_op jit(solution)/shard_map/psum | solution.py:269
  (433 shorter events, 303.0 us)
Async XLA Ops:
  7.2 22.9 %copy-start.11 = (bf16[2,256,960]{1,2,0:T(8,128)(2,1)S(1)}, bf16[2,256,960]{1,2,0:T(8,128)(2,1)}, u32[]{:S(2)}) copy-start(bf16[2,256,960]{1,2,0:T(8,128)(2,1)} %param.16) | copy-start | bytes 2949124
  7.2 22.9 %all-gather.12.cloned.1.call-start = ((), (), s32[]{:S(2)}) async-start(), calls=%async_computation.6 | async-start | bytes 1536000 | tf_op jit(solution)/shard_map/all_gather | solution.py:125
  7.9 45.6 %all-gather.10.cloned.1.call-start = ((), (), s32[]{:S(2)}) async-start(), calls=%async_computation.5 | async-start | bytes 2457600 | tf_op jit(solution)/shard_map/all_gather | solution.py:124
  8.7 133.9 %all-gather.14.cloned.1.call-start = ((), (), s32[]{:S(2)}) async-start(), calls=%async_computation.7 | async-start | bytes 5898240 | tf_op jit(solution)/shard_map/all_gather | solution.py:142
  20.8 32.8 %copy-start.28 = (f32[960]{0:T(1024)}, f32[960]{0:T(1024)S(1)}, u32[]{:S(2)}) copy-start(f32[960]{0:T(1024)S(1)} %convert_element_type.123) | copy-start | bytes 11524
  22.2 31.3 %copy-start.31 = (f32[2,256]{1,0:T(2,128)}, f32[2,256]{1,0:T(2,128)S(1)}, u32[]{:S(2)}) copy-start(f32[2,256]{1,0:T(2,128)S(1)} %add_rsqrt_fusion.1) | copy-start | bytes 6148
  23.0 33.4 %copy-start.21 = (f32[256,32]{0,1:T(8,128)}, f32[256,32]{0,1:T(8,128)S(1)}, u32[]{:S(2)}) copy-start(f32[256,32]{0,1:T(8,128)S(1)} %get-tuple-element.374) | copy-start | bytes 98308
  34.4 208.9 %all-gather.16.cloned.1.call-start = ((), (), s32[]{:S(2)}) async-start(), calls=%async_computation.8 | async-start | bytes 2457600 | tf_op jit(solution)/shard_map/all_gather | solution.py:126
  35.0 213.7 %all-gather.26.cloned.1.call-start = ((), (), s32[]{:S(2)}) async-start(), calls=%async_computation.14 | async-start | bytes 2949120 | tf_op jit(solution)/shard_map/all_gather | solution.py:168
  35.6 213.1 %all-gather.24.cloned.1.call-start = ((), (), s32[]{:S(2)}) async-start(), calls=%async_computation.12 | async-start | bytes 3072000 | tf_op jit(solution)/shard_map/all_gather | solution.py:160
  36.2 220.1 %all-gather.22.cloned.1.call-start = ((), (), s32[]{:S(2)}) async-start(), calls=%async_computation.11 | async-start | bytes 3072000 | tf_op jit(solution)/shard_map/all_gather | solution.py:159
  36.9 246.2 %all-gather.18.cloned.1.call-start = ((), (), s32[]{:S(2)}) async-start(), calls=%async_computation.9 | async-start | bytes 2949120 | tf_op jit(solution)/shard_map/all_gather | solution.py:167
  150.6 7.3 copy-start.18
  247.7 61.7 %all-gather.20.cloned.1.call-start = ((), (), s32[]{:S(2)}) async-start(), calls=%async_computation.10 | async-start | bytes 3072000 | tf_op jit(solution)/shard_map/all_gather | solution.py:158
  248.5 133.4 %reduce-scatter.8.cloned.1.call-start = ((), (), s32[]{:S(2)}) async-start(), calls=%async_computation.15 | async-start | bytes 5898240 | tf_op jit(solution)/shard_map/reduce_scatter | solution.py:193
  309.4 11.9 %copy-start.33 = (bf16[960,1280]{1,0:T(8,128)(2,1)S(1)}, bf16[960,1280]{1,0:T(8,128)(2,1)}, u32[]{:S(2)}) copy-start(bf16[960,1280]{1,0:T(8,128)(2,1)} %all-gather.22.cloned.1.call-done) | copy-start | bytes 7372804
  321.3 3.5 copy-start.34
  329.7 84.9 %reduce-scatter.6.cloned.1.call-start = ((), (), s32[]{:S(2)}) async-start(), calls=%async_computation.13 | async-start | bytes 2949120 | tf_op jit(solution)/shard_map/reduce_scatter | solution.py:176
  336.4 5.6 copy-start.36
  336.4 5.6 copy-start.41
  342.0 3.5 copy-start.39
  352.2 62.4 %copy-start.10 = (bf16[2,256,960]{1,2,0:T(8,128)(2,1)S(1)}, bf16[2,256,960]{1,2,0:T(8,128)(2,1)}, u32[]{:S(2)}) copy-start(bf16[2,256,960]{1,2,0:T(8,128)(2,1)} %param.17) | copy-start | bytes 2949124
  414.6 3.5 copy-start.35
  421.6 168.5 %reduce-scatter.14.cloned.1.call-start = ((), (), s32[]{:S(2)}) async-start(), calls=%async_computation.20 | async-start | bytes 2949120 | tf_op jit(solution)/shard_map/while/body/eval_jaxpr/reduce_scatter | solution.py:215
  445.8 2.9 copy-start.3
  461.7 2.9 copy-start.3
  477.7 2.9 copy-start.3
  493.7 2.9 copy-start.3
  496.6 2.9 copy-start.1
  509.7 2.9 copy-start.3
  512.6 2.8 copy-start.1
  519.0 71.1 %copy-start.13 = (f32[2,256,640]{1,2,0:T(8,128)S(1)}, f32[2,256,640]{1,2,0:T(8,128)}, u32[]{:S(2)}) copy-start(f32[2,256,640]{1,2,0:T(8,128)} %get-tuple-element.691) | copy-start | bytes 3932164 | tf_op jit(solution)/shard_map/while
  592.2 167.1 %reduce-scatter.14.cloned.1.call-start = ((), (), s32[]{:S(2)}) async-start(), calls=%async_computation.20 | async-start | bytes 2949120 | tf_op jit(solution)/shard_map/while/body/eval_jaxpr/reduce_scatter | solution.py:215
  616.3 2.9 copy-start.3
  619.3 2.9 copy-start.1
  632.3 2.9 copy-start.3
  648.2 2.9 copy-start.3
  664.2 2.9 copy-start.3
  667.1 2.9 copy-start.1
  680.2 2.9 copy-start.3
  689.5 69.8 %copy-start.13 = (f32[2,256,640]{1,2,0:T(8,128)S(1)}, f32[2,256,640]{1,2,0:T(8,128)}, u32[]{:S(2)}) copy-start(f32[2,256,640]{1,2,0:T(8,128)} %get-tuple-element.691) | copy-start | bytes 3932164 | tf_op jit(solution)/shard_map/while
  761.4 67.7 %reduce-scatter.12.cloned.1.call-start = ((), (), s32[]{:S(2)}) async-start(), calls=%async_computation.18 | async-start | bytes 9216000 | tf_op jit(solution)/shard_map/reduce_scatter | solution.py:278
  761.9 119.0 %reduce-scatter.10.cloned.1.call-start = ((), (), s32[]{:S(2)}) async-start(), calls=%async_computation.16 | async-start | bytes 6144000 | tf_op jit(solution)/shard_map/reduce_scatter | solution.py:275
  789.0 172.6 %all-reduce.12.cloned.1.call-start = ((), (), s32[]{:S(2)}) async-start(), calls=%async_computation.19 | async-start | bytes 3686400 | tf_op jit(solution)/shard_map/psum | solution.py:273
  829.1 216.1 %all-reduce.10.cloned.1.call-start = ((), (), s32[]{:S(2)}) async-start(), calls=%async_computation.17 | async-start | bytes 2457600 | tf_op jit(solution)/shard_map/psum | solution.py:269
  829.8 3.2 copy-start.24
  829.8 3.1 copy-start.26
  829.8 3.1 copy-start.37
  (59 other events, 105.7 us)
Sparse Core Ops, SparseCore 0:
  9.6 20.4 all-gather.11
  31.6 21.8 all-gather.9
  56.3 86.2 all-gather.13
  144.0 20.0 all-gather.15
  165.4 31.5 all-gather.25
  198.5 24.6 all-gather.23
  224.8 24.5 all-gather.21
  251.5 31.5 all-gather.17
  284.7 24.6 all-gather.19
  329.8 51.9 reduce-scatter.7
  384.2 30.3 reduce-scatter.5
  519.1 70.9 reduce-scatter.13
  689.7 69.5 reduce-scatter.13
  764.4 64.6 reduce-scatter.11
  831.7 49.1 reduce-scatter.9
  883.2 78.4 all-reduce.11
  965.0 80.1 all-reduce.9
where the time goes:
time: 1060 us
  waiting for transfers between devices  568 us (54%)
  matrix products  260 us (25%)
  local copies, waits for them, and re-layouts  112 us (11%)
  other arithmetic  60.4 us (6%)
  blocking collectives  35.6 us (3%)
  between operations  16 us (2%)
    reduce_scatter x2, waiting for transfers between devices, attend_back(): lax.psum_scatter(back_keyval.astype(jnp.bfloat16), ('ctx', 'tp'), scatter...  136 us
    all_gather x1, waiting for transfers between devices, on_device(): lax.all_gather(keyval_low, ('ctx', 'tp'), axis=1, tiled=True)  84 us
    psum x1, waiting for transfers between devices, on_device(): lax.psum(attention_term.astype(jnp.bfloat16), ('ctx', 'tp'))  80.2 us
    psum x1, waiting for transfers between devices, on_device(): feed_total = lax.psum(feed_term.astype(jnp.bfloat16), 'ctx')  77.4 us
    dot_general x20, matrix products, masked_scores(): jnp.einsum('qd,kd->qk', query_group, key_group, preferred_element_type=jn...  60.3 us
    reduce_scatter x1, waiting for transfers between devices, on_device(): lax.psum_scatter(feed_total, 'fsdp', scatter_dimension=0, tiled=True)  40 us
    dot_general x10, matrix products, head_forward(): jnp.einsum('qk,kd->qd', weights, value_group, preferred_element_type=jnp....  33.4 us
    reduce_scatter x1, waiting for transfers between devices, on_device(): lax.psum_scatter(branch_part.astype(jnp.bfloat16), 'tp', scatter_dimensio...  30.1 us
  transfers between devices with their start and end apart: 17, of which 13 were waited for; matrix products, arithmetic and copies ran while one was open for 19% of the time, Pallas kernels for 0%

commit v1 on v0

--- a/solution.py
+++ b/solution.py
@@ -266,7 +266,7 @@
     attention_term = jnp.concatenate([grad_query, grad_keyval, grad_output], 1)
     feed_term = jnp.concatenate([grad_gate, grad_up, grad_down], 1)
     attention_total, gain_one_total, gain_two_total = (
-        lax.psum(attention_term.astype(jnp.bfloat16), ("ctx", "tp")).astype(jnp.float32),
+        lax.psum(lax.psum(attention_term.astype(jnp.bfloat16), "tp"), "ctx").astype(jnp.float32),
         lax.psum(grad_gain_one.astype(jnp.bfloat16), ("ctx", "tp")).astype(jnp.float32),
         lax.psum(grad_gain_two.astype(jnp.bfloat16), ("ctx", "tp")).astype(jnp.float32),
     )

time: 1060 us -> 1090 us (1.028)
  waiting for transfers between devices: 568 us -> 598 us
    psum x2, waiting for transfers between devices: 158 us -> 129 us  [the longest x1 82.8 us: on_device(): lax.psum(lax.psum(attention_term.astype(jnp.bfloat16), 'tp'), 'ctx')]
    reduce_scatter x1, waiting for transfers between devices: 40 us -> 68.2 us  [on_device(): lax.psum_scatter(feed_total, 'fsdp', scatter_dimension=0, tiled=True)]
    reduce_scatter x1, waiting for transfers between devices: 29.6 us -> 45.5 us  [on_device(): lax.psum_scatter(back_normed_part, 'tp', scatter_dimension=1, tiled=True)]
    reduce_scatter x1, waiting for transfers between devices: 16.8 us -> 31.6 us  [on_device(): lax.psum_scatter(attention_total.astype(jnp.bfloat16), 'fsdp', scatter_di...]
  transfers between devices with their start and end apart: 17 -> 17, of which waited for: 13 -> 13; matrix products, arithmetic and copies ran while one was open for 19% -> 16% of each run, Pallas kernels for 0% -> 0%
where the time goes in v1:
time: 1090 us
  waiting for transfers between devices  598 us (55%)
  matrix products  261 us (24%)
  local copies, waits for them, and re-layouts  113 us (10%)
  other arithmetic  60.1 us (6%)
  blocking collectives  36.7 us (3%)
  between operations  16 us (1%)
    reduce_scatter x2, waiting for transfers between devices, attend_back(): lax.psum_scatter(back_keyval.astype(jnp.bfloat16), ('ctx', 'tp'), scatter...  137 us
    all_gather x1, waiting for transfers between devices, on_device(): lax.all_gather(keyval_low, ('ctx', 'tp'), axis=1, tiled=True)  84 us
    psum x1, waiting for transfers between devices, on_device(): lax.psum(lax.psum(attention_term.astype(jnp.bfloat16), 'tp'), 'ctx')  82.8 us
    reduce_scatter x1, waiting for transfers between devices, on_device(): lax.psum_scatter(feed_total, 'fsdp', scatter_dimension=0, tiled=True)  68.2 us
    dot_general x20, matrix products, masked_scores(): jnp.einsum('qd,kd->qk', query_group, key_group, preferred_element_type=jn...  60.2 us
    psum x1, waiting for transfers between devices, on_device(): lax.psum(attention_term.astype(jnp.bfloat16), 'tp')  46.1 us
    reduce_scatter x1, waiting for transfers between devices, on_device(): lax.psum_scatter(back_normed_part, 'tp', scatter_dimension=1, tiled=True)  45.5 us
    dot_general x10, matrix products, head_forward(): jnp.einsum('qk,kd->qd', weights, value_group, preferred_element_type=jnp....  33.4 us
  transfers between devices with their start and end apart: 17, of which 13 were waited for; matrix products, arithmetic and copies ran while one was open for 16% of the time, Pallas kernels for 0%

profile of v1, /device:TPU:0, one launch (start us, length us, event | category | flops | bytes accessed | tf_op | source)
XLA Modules:
  0.0 1086.8 jit_solution(14684172461169726925)
XLA Ops:
  12.4 8.3 all-reduce.7
  23.0 7.0 all-gather.12.cloned.1.call-done
  37.2 16.3 %all-gather.10.cloned.1.call-done = bf16[960,960]{1,0:T(8,128)(2,1)} async-done(((bf16[240,960]{1,0:T(8,128)(2,1)}), bf16[960,960]{1,0:T(8,128)(2,1)}) %all-gather.10.cloned.1.call-update) | async-done | bytes 1843216 | tf_op jit(solution)/shard_map/all_gather | solution.py:124
  58.6 84.0 %all-gather.14.cloned.1.call-done = bf16[2,2048,640]{2,1,0:T(8,128)(2,1)} async-done(((bf16[2,256,640]{2,1,0:T(8,128)(2,1)}), bf16[2,2048,640]{2,1,0:T(8,128)(2,1)}) %all-gather.14.cloned.1.call-update) | async-done | bytes 5242896 | tf_op jit(solution)/shard_map/all_gather | solution.py:142
  142.6 8.0 copy.72
  150.6 7.4 slice_bitcast_fusion
  158.0 80.5 %while.43 = (s32[]{:T(128)}, bf16[10,768,64]{1,2,0:T(8,128)(2,1)S(1)}, f32[10,768]{1,0:T(8,128)S(1)}, f32[10,768]{1,0:T(8,128)S(1)}, bf16[10,768,64]{2,1,0:T(8,1...) while((s32[]{:T(128)}, ...), condition=%wide.region_4.5_spmd.clone, body=%wide.region_1.4_spmd.clone.sunk | while | flops 426244608 | bytes 19846260 | solution.py:151
  170.5 3.4 fusion.152
  210.8 3.3 fusion.152
  249.0 7.6 fusion.58
  256.6 26.6 %all-gather.18.cloned.1.call-done = bf16[2,512,960]{1,2,0:T(8,128)(2,1)} async-done(((bf16[2,256,960]{1,2,0:T(8,128)(2,1)}), bf16[2,512,960]{1,2,0:T(8,128)(2,1)}) %all-gather.18.cloned.1.call-update) | async-done | bytes 1966096 | tf_op jit(solution)/shard_map/all_gather | solution.py:167
  283.1 7.6 fusion.64
  290.8 18.6 %all-gather.20.cloned.1.call-done = bf16[960,1280]{1,0:T(8,128)(2,1)} async-done(((bf16[240,1280]{1,0:T(8,128)(2,1)}), bf16[960,1280]{1,0:T(8,128)(2,1)}) %all-gather.20.cloned.1.call-update) | async-done | bytes 2457616 | tf_op jit(solution)/shard_map/all_gather | solution.py:158
  309.4 12.0 %multiply_convert_fusion.2 = (bf16[2,512,1280]{2,1,0:T(8,128)(2,1)S(1)}, bf16[2,512,1280]{2,1,0:T(8,128)(2,1)S(1)}, bf16[2,512,1280]{2,1,0:T(8,128)(2,1)}) fusion(f32[2,512,1280]{2,1,0:T(8,128)} %fusion.58, f32[2,512,1280]{2,1,0:T(8,128)} %fusion.64, bf16[2,512,960]{1,2,0:T(8,128)(2,1)} %all-gather.18.cloned.1.call-done, ...), kind=kOutput, calls=%fused_computation.71 | convolution fusion | flops 2536243200 | bytes 22773760 | tf_op jit(solution)/shard_map/dot_general | solution.py:170
  324.9 4.9 fusion.85
  329.8 6.5 fusion.88
  336.4 45.5 %reduce-scatter.8.cloned.1.call-done = f32[2,256,960]{1,2,0:T(8,128)} async-done(((f32[2,512,960]{1,2,0:T(8,128)}), f32[2,256,960]{1,2,0:T(8,128)}) %reduce-scatter.8.cloned.1.call-update) | async-done | bytes 1966096 | tf_op jit(solution)/shard_map/reduce_scatter | solution.py:193
  384.6 30.0 %reduce-scatter.6.cloned.1.call-done = bf16[2,256,960]{1,2,0:T(8,128)(2,1)} async-done(((bf16[2,512,960]{1,2,0:T(8,128)(2,1)}), bf16[2,256,960]{1,2,0:T(8,128)(2,1)}) %reduce-scatter.6.cloned.1.call-update) | async-done | bytes 983056 | tf_op jit(solution)/shard_map/reduce_scatter | solution.py:176
  414.7 3.5 multiply_add_fusion
  421.2 340.5 %while.45 = (s32[]{:T(128)}, f32[2,5,768,64]{2,3,1,0:T(8,128)}, f32[2,256,640]{1,2,0:T(8,128)}, bf16[2,5,768,64]{3,2,1,0:T(8,128)(2,1)}, bf16[2,5,2048,64]{2,3,1...) while((s32[]{:T(128)}, f32[2,5,768,64]{2,3,1,0:T(8,128)}, ...), condition=%wide.region_14.15_spmd.clone, body=%wide.region_9.14_spmd.clone.sunk | while | flops 1025588480 | bytes 125203080 | solution.py:233
  435.0 80.2 %while.46 = (s32[]{:T(128)}, f32[5,768,64]{1,2,0:T(8,128)}, bf16[5,2048,64]{1,2,0:T(8,128)(2,1)}, bf16[5,2048,64]{1,2,0:T(8,128)(2,1)}, bf16[5,768,64]{2,1,0:T(8...) while((s32[]{:T(128)}, f32[5,768,64]{1,2,0:T(8,128)}, ...), condition=%wide.region_12.12_spmd, body=%wide.region_10.11_spmd.sunk | while | flops 1022541056 | bytes 79656208 | solution.py:207
  438.6 3.7 multiply_reduce_fusion.5
  454.7 3.7 multiply_reduce_fusion.5
  470.7 3.7 multiply_reduce_fusion.5
  486.7 3.7 multiply_reduce_fusion.5
  502.8 3.7 multiply_reduce_fusion.5
  515.3 3.4 pad_maximum_fusion.11
  520.9 68.9 %reduce-scatter.14.cloned.1.call-done = bf16[256,640]{0,1:T(8,128)(2,1)} async-done(((bf16[2048,640]{0,1:T(8,128)(2,1)}), bf16[256,640]{0,1:T(8,128)(2,1)}) %reduce-scatter.14.cloned.1.call-update) | async-done | bytes 327696 | tf_op jit(solution)/shard_map/while/body/eval_jaxpr/reduce_scatter | solution.py:215
  605.9 80.3 %while.46 = (s32[]{:T(128)}, f32[5,768,64]{1,2,0:T(8,128)}, bf16[5,2048,64]{1,2,0:T(8,128)(2,1)}, bf16[5,2048,64]{1,2,0:T(8,128)(2,1)}, bf16[5,768,64]{2,1,0:T(8...) while((s32[]{:T(128)}, f32[5,768,64]{1,2,0:T(8,128)}, ...), condition=%wide.region_12.12_spmd, body=%wide.region_10.11_spmd.sunk | while | flops 1022541056 | bytes 79656208 | solution.py:207
  609.5 3.7 multiply_reduce_fusion.5
  625.5 3.7 multiply_reduce_fusion.5
  641.6 3.7 multiply_reduce_fusion.5
  657.6 3.7 multiply_reduce_fusion.5
  673.7 3.7 multiply_reduce_fusion.5
  686.1 3.4 pad_maximum_fusion.11
  691.8 67.7 %reduce-scatter.14.cloned.1.call-done = bf16[256,640]{0,1:T(8,128)(2,1)} async-done(((bf16[2048,640]{0,1:T(8,128)(2,1)}), bf16[256,640]{0,1:T(8,128)(2,1)}) %reduce-scatter.14.cloned.1.call-update) | async-done | bytes 327696 | tf_op jit(solution)/shard_map/while/body/eval_jaxpr/reduce_scatter | solution.py:215
  765.4 3.7 bitcast_convert_fusion.3
  780.6 8.6 concatenate.38
  790.8 4.8 fusion.53
  795.6 3.4 bitcast_convert_fusion.2
  799.1 3.4 bitcast_convert_fusion.1
  802.5 3.4 pad_maximum_fusion.1
  806.0 31.6 %reduce-scatter.12.cloned.1.call-done = bf16[240,2560]{1,0:T(8,128)(2,1)} async-done(((bf16[960,2560]{1,0:T(8,128)(2,1)}), bf16[240,2560]{1,0:T(8,128)(2,1)}) %reduce-scatter.12.cloned.1.call-update) | async-done | bytes 1228816 | tf_op jit(solution)/shard_map/reduce_scatter | solution.py:275
  837.6 68.2 %reduce-scatter.10.cloned.1.call-done = bf16[240,3840]{1,0:T(8,128)(2,1)} async-done(((bf16[960,3840]{1,0:T(8,128)(2,1)}), bf16[240,3840]{1,0:T(8,128)(2,1)}) %reduce-scatter.10.cloned.1.call-update) | async-done | bytes 1843216 | tf_op jit(solution)/shard_map/reduce_scatter | solution.py:278
  905.8 46.1 %all-reduce.11.cloned.1.call-done = bf16[240,2560]{1,0:T(8,128)(2,1)} async-done(((bf16[240,2560]{1,0:T(8,128)(2,1)}), bf16[240,2560]{1,0:T(8,128)(2,1)}) %all-reduce.11.cloned.1.call-update) | async-done | bytes 1228816 | tf_op jit(solution)/shard_map/psum | solution.py:269
  958.1 7.0 all-reduce.6
  965.3 21.4 %all-reduce.4 = (bf16[240]{0:T(256)(128)(2,1)S(1)}, bf16[240]{0:T(256)(128)(2,1)S(1)}) all-reduce(bf16[240]{0:T(256)(128)(2,1)S(1)} %dynamic-slice.3, bf16[240]{0:T(256)(128)(2,1)S(1)} %dynamic-slice.5), channel_id=1, replica_groups=mesh['fsdp'=4,'ctx'=4,'tp'=2] {'ctx','tp'}, use_global_device_ids=true, to_apply=%region_17.18 | all-reduce | flops 480 | bytes 1920 | tf_op jit(solution)/shard_map/psum | solution.py:270
  991.1 82.8 %all-reduce.13.cloned.1.call-done = (bf16[240,2560]{1,0:T(8,128)(2,1)}, bf16[240,3840]{1,0:T(8,128)(2,1)}) async-done(((bf16[240,2560]{1,0:T(8,128)(2,1)}, bf16[240,3840]{1,0:T(8,128)(2,1)}), (bf16[240,2560]{1,0:T(8,128)(2,1)}, bf16[240,3840]{1,0:T(8,128)(2,1)})) %all-reduce.13.cloned.1.call-update) | async-done | bytes 3072016 | tf_op jit(solution)/shard_map/psum | solution.py:269
  (435 shorter events, 304.3 us)
Async XLA Ops:
  7.2 22.9 %copy-start.12 = (bf16[2,256,960]{1,2,0:T(8,128)(2,1)S(1)}, bf16[2,256,960]{1,2,0:T(8,128)(2,1)}, u32[]{:S(2)}) copy-start(bf16[2,256,960]{1,2,0:T(8,128)(2,1)} %param.16) | copy-start | bytes 2949124
  7.2 22.9 %all-gather.12.cloned.1.call-start = ((), (), s32[]{:S(2)}) async-start(), calls=%async_computation.6 | async-start | bytes 1536000 | tf_op jit(solution)/shard_map/all_gather | solution.py:125
  7.9 45.6 %all-gather.10.cloned.1.call-start = ((), (), s32[]{:S(2)}) async-start(), calls=%async_computation.5 | async-start | bytes 2457600 | tf_op jit(solution)/shard_map/all_gather | solution.py:124
  8.7 133.9 %all-gather.14.cloned.1.call-start = ((), (), s32[]{:S(2)}) async-start(), calls=%async_computation.7 | async-start | bytes 5898240 | tf_op jit(solution)/shard_map/all_gather | solution.py:142
  20.8 32.8 %copy-start.28 = (f32[960]{0:T(1024)}, f32[960]{0:T(1024)S(1)}, u32[]{:S(2)}) copy-start(f32[960]{0:T(1024)S(1)} %convert_element_type.123) | copy-start | bytes 11524
  22.2 31.3 %copy-start.31 = (f32[2,256]{1,0:T(2,128)}, f32[2,256]{1,0:T(2,128)S(1)}, u32[]{:S(2)}) copy-start(f32[2,256]{1,0:T(2,128)S(1)} %add_rsqrt_fusion.1) | copy-start | bytes 6148
  23.0 33.4 %copy-start.22 = (f32[256,32]{0,1:T(8,128)}, f32[256,32]{0,1:T(8,128)S(1)}, u32[]{:S(2)}) copy-start(f32[256,32]{0,1:T(8,128)S(1)} %get-tuple-element.376) | copy-start | bytes 98308
  34.4 209.0 %all-gather.16.cloned.1.call-start = ((), (), s32[]{:S(2)}) async-start(), calls=%async_computation.8 | async-start | bytes 2457600 | tf_op jit(solution)/shard_map/all_gather | solution.py:126
  35.0 214.0 %all-gather.26.cloned.1.call-start = ((), (), s32[]{:S(2)}) async-start(), calls=%async_computation.14 | async-start | bytes 2949120 | tf_op jit(solution)/shard_map/all_gather | solution.py:168
  35.6 213.4 %all-gather.24.cloned.1.call-start = ((), (), s32[]{:S(2)}) async-start(), calls=%async_computation.12 | async-start | bytes 3072000 | tf_op jit(solution)/shard_map/all_gather | solution.py:160
  36.2 220.4 %all-gather.22.cloned.1.call-start = ((), (), s32[]{:S(2)}) async-start(), calls=%async_computation.11 | async-start | bytes 3072000 | tf_op jit(solution)/shard_map/all_gather | solution.py:159
  36.9 246.2 %all-gather.18.cloned.1.call-start = ((), (), s32[]{:S(2)}) async-start(), calls=%async_computation.9 | async-start | bytes 2949120 | tf_op jit(solution)/shard_map/all_gather | solution.py:167
  150.6 7.4 copy-start.20
  247.8 61.6 %all-gather.20.cloned.1.call-start = ((), (), s32[]{:S(2)}) async-start(), calls=%async_computation.10 | async-start | bytes 3072000 | tf_op jit(solution)/shard_map/all_gather | solution.py:158
  248.5 133.4 %reduce-scatter.8.cloned.1.call-start = ((), (), s32[]{:S(2)}) async-start(), calls=%async_computation.15 | async-start | bytes 5898240 | tf_op jit(solution)/shard_map/reduce_scatter | solution.py:193
  309.4 12.0 %copy-start.33 = (bf16[960,1280]{1,0:T(8,128)(2,1)S(1)}, bf16[960,1280]{1,0:T(8,128)(2,1)}, u32[]{:S(2)}) copy-start(bf16[960,1280]{1,0:T(8,128)(2,1)} %all-gather.22.cloned.1.call-done) | copy-start | bytes 7372804
  321.4 3.5 copy-start.34
  329.8 84.9 %reduce-scatter.6.cloned.1.call-start = ((), (), s32[]{:S(2)}) async-start(), calls=%async_computation.13 | async-start | bytes 2949120 | tf_op jit(solution)/shard_map/reduce_scatter | solution.py:176
  336.4 78.2 %copy-start.11 = (bf16[2,256,960]{1,2,0:T(8,128)(2,1)S(1)}, bf16[2,256,960]{1,2,0:T(8,128)(2,1)}, u32[]{:S(2)}) copy-start(bf16[2,256,960]{1,2,0:T(8,128)(2,1)} %param.17) | copy-start | bytes 2949124
  414.7 3.5 copy-start.37
  421.2 168.7 %reduce-scatter.14.cloned.1.call-start = ((), (), s32[]{:S(2)}) async-start(), calls=%async_computation.20 | async-start | bytes 2949120 | tf_op jit(solution)/shard_map/while/body/eval_jaxpr/reduce_scatter | solution.py:215
  445.3 2.9 copy-start.3
  461.3 2.9 copy-start.3
  477.4 2.9 copy-start.3
  493.4 2.9 copy-start.3
  496.3 2.9 copy-start.1
  509.5 2.9 copy-start.3
  512.4 2.9 copy-start.1
  518.7 71.2 %copy-start.14 = (f32[2,256,640]{1,2,0:T(8,128)S(1)}, f32[2,256,640]{1,2,0:T(8,128)}, u32[]{:S(2)}) copy-start(f32[2,256,640]{1,2,0:T(8,128)} %get-tuple-element.693) | copy-start | bytes 3932164 | tf_op jit(solution)/shard_map/while
  592.0 167.4 %reduce-scatter.14.cloned.1.call-start = ((), (), s32[]{:S(2)}) async-start(), calls=%async_computation.20 | async-start | bytes 2949120 | tf_op jit(solution)/shard_map/while/body/eval_jaxpr/reduce_scatter | solution.py:215
  616.1 2.9 copy-start.3
  632.2 2.9 copy-start.3
  648.2 2.9 copy-start.3
  664.3 2.9 copy-start.3
  667.2 2.9 copy-start.1
  680.3 2.9 copy-start.3
  683.3 2.9 copy-start.1
  689.5 69.9 %copy-start.14 = (f32[2,256,640]{1,2,0:T(8,128)S(1)}, f32[2,256,640]{1,2,0:T(8,128)}, u32[]{:S(2)}) copy-start(f32[2,256,640]{1,2,0:T(8,128)} %get-tuple-element.693) | copy-start | bytes 3932164 | tf_op jit(solution)/shard_map/while
  761.7 3.7 copy-start.7
  761.7 75.9 %reduce-scatter.12.cloned.1.call-start = ((), (), s32[]{:S(2)}) async-start(), calls=%async_computation.17 | async-start | bytes 6144000 | tf_op jit(solution)/shard_map/reduce_scatter | solution.py:275
  789.3 116.6 %reduce-scatter.10.cloned.1.call-start = ((), (), s32[]{:S(2)}) async-start(), calls=%async_computation.16 | async-start | bytes 9216000 | tf_op jit(solution)/shard_map/reduce_scatter | solution.py:278
  790.8 4.8 copy-start.36
  790.8 4.8 copy-start.42
  795.6 3.5 copy-start.40
  805.9 146.1 %all-reduce.11.cloned.1.call-start = ((), (), s32[]{:S(2)}) async-start(), calls=%async_computation.18 | async-start | bytes 2457600 | tf_op jit(solution)/shard_map/psum | solution.py:269
  837.6 115.1 %copy-start.19 = (bf16[2,256,15,64]{1,3,2,0:T(8,128)(2,1)S(1)}, bf16[2,256,15,64]{1,3,2,0:T(8,128)(2,1)}, u32[]{:S(2)}) copy-start(bf16[2,256,15,64]{1,3,2,0:T(8,128)(2,1)} %copy-done.18) | copy-start | bytes 2949124
  837.6 236.3 %all-reduce.13.cloned.1.call-start = ((), (), s32[]{:S(2)}) async-start(), calls=%async_computation.19 | async-start | bytes 6144000 | tf_op jit(solution)/shard_map/psum | solution.py:269
  955.6 32.2 %copy-start.8 = (f32[2,256,960]{1,2,0:T(8,128)S(1)}, f32[2,256,960]{1,2,0:T(8,128)}, u32[]{:S(2)}) copy-start(f32[2,256,960]{1,2,0:T(8,128)} %copy-done.6) | copy-start | bytes 5898244
  (60 other events, 108.8 us)
Sparse Core Ops, SparseCore 0:
  9.6 20.4 all-gather.11
  31.6 21.8 all-gather.9
  56.3 86.2 all-gather.13
  144.0 20.0 all-gather.15
  165.4 31.5 all-gather.25
  198.5 24.7 all-gather.23
  224.8 24.5 all-gather.21
  251.5 31.6 all-gather.17
  284.7 24.6 all-gather.19
  329.9 51.9 reduce-scatter.7
  384.3 30.3 reduce-scatter.5
  518.8 71.0 reduce-scatter.13
  689.7 69.7 reduce-scatter.13
  789.4 48.1 reduce-scatter.11
  840.1 65.6 reduce-scatter.9
  908.0 43.9 all-reduce.10
  954.5 119.3 all-reduce.12
